TPU v7x, 128 devices: a whole 4x4x4 slice. The times are simulated.
128 devices in a mesh: tm: 16 (over x, z), head: 8 (over y, core).
Axes of the slice: x: 4, y: 4, z: 4, core: 2. Of those that a mesh axis runs over, the one named last changes fastest.
Arguments:
- query_in: bfloat16 [12544, 5120], P('tm', 'head'), may hold values from -6 to 6
- key_in: bfloat16 [12544, 5120], P('tm', 'head'), may hold values from -6 to 6
- value_in: bfloat16 [12544, 5120], P('tm', 'head'), may hold values from -6 to 6
- layer_grad: bfloat16 [12544, 5120], P('tm', 'head'), may hold values from -6 to 6
- out_weight: bfloat16 [5120, 5120], P('head'), may hold values from -0.078125 to 0.078125
- group_mask: int32 [16, 16], replicated, may hold values from 0 to 1, as said below
- first_group: int32 [1], replicated, may hold values from 0 to 15
Outputs:
- query_grad: bfloat16 [12544, 5120], P('tm', 'head')
- key_grad: bfloat16 [12544, 5120], P('tm', 'head')
- value_grad: bfloat16 [12544, 5120], P('tm', 'head')
Inputs may be any that keep to these rules, and one draw needn't show every extreme that they name: `group_mask`: 1 on the diagonal; each entry just below the diagonal is 1 or 0; every other entry is 0.
All inputs are finite; a program needn't handle non-finite values.
Results may differ from a plain program's by a relative error of at most 0.015.
Values may be sent and summed in bfloat16 or wider, within the bound.
A program may use at most 192 MiB of HBM per device.

v0:
```python
import jax
import jax.numpy as jnp
from jax import lax
from jax.sharding import PartitionSpec as P

D_HEAD = 128


lowest_start = -1e30


def from_root(shard, axis, root):
    mine = lax.axis_index(axis) == root
    return lax.psum(jnp.where(mine, shard, jnp.zeros_like(shard)), axis)


def passed_along(block, axis, distance):
    devices = range(lax.axis_size(axis))
    route = [(i - distance, i) for i in devices if i - distance in devices]
    return lax.ppermute(block, axis, route)


def split_heads(block, head_dim):
    return block.reshape(block.shape[0], block.shape[1] // head_dim, head_dim)


def empty_stats(heads, rows):
    return (
        jnp.full((heads, rows), lowest_start, jnp.float32),
        jnp.zeros((heads, rows), jnp.float32),
        jnp.zeros((heads, rows), jnp.float32),
    )


def pair_stats(query_blk, grad_blk, key_blk, value_blk, scale):
    scores = scale * jnp.einsum(
        "qhd,khd->hqk", query_blk, key_blk, preferred_element_type=jnp.float32
    )
    peak = jnp.max(scores, axis=2)
    weights = jnp.exp(scores - peak[:, :, None])
    dprobs = jnp.einsum("qhd,khd->hqk", grad_blk, value_blk, preferred_element_type=jnp.float32)
    return (peak, jnp.sum(weights, axis=2), jnp.sum(weights * dprobs, axis=2))


def merge_stats(left, right):
    top = jnp.maximum(left[0], right[0])
    left_f = jnp.exp(left[0] - top)
    right_f = jnp.exp(right[0] - top)
    return (top, left[1] * left_f + right[1] * right_f, left[2] * left_f + right[2] * right_f)


def pair_grads(query_blk, grad_blk, log_sums, deltas, key_blk, value_blk, scale):
    scores = scale * jnp.einsum(
        "qhd,khd->hqk", query_blk, key_blk, preferred_element_type=jnp.float32
    )
    probs = jnp.exp(scores - log_sums[:, :, None])
    probs_low = probs.astype(jnp.bfloat16)
    value_term = jnp.einsum("hqk,qhd->khd", probs_low, grad_blk, preferred_element_type=jnp.float32)
    dprobs = jnp.einsum("qhd,khd->hqk", grad_blk, value_blk, preferred_element_type=jnp.float32)
    dscores = (probs * (dprobs - deltas[:, :, None])).astype(jnp.bfloat16)
    query_term = scale * jnp.einsum(
        "hqk,khd->qhd", dscores, key_blk, preferred_element_type=jnp.float32
    )
    key_term = scale * jnp.einsum(
        "hqk,qhd->khd", dscores, query_blk, preferred_element_type=jnp.float32
    )
    return (query_term, key_term, value_term)


def local(query_in, key_in, value_in, layer_grad, out_weight, group_mask, first_group):
    rows_loc, width_loc = query_in.shape
    head_dim = D_HEAD
    heads_loc = width_loc // head_dim
    scale = head_dim ** (-0.5)
    my_dev = lax.axis_index("tm")
    first = first_group[0]
    attn_grad = lax.dot_general(
        lax.all_gather(layer_grad, "head", axis=1, tiled=True),
        out_weight,
        (((1,), (1,)), ((), ())),
        preferred_element_type=jnp.float32,
    ).astype(jnp.bfloat16)
    query_three = split_heads(query_in, head_dim)
    grad_three = split_heads(attn_grad, head_dim)
    key_three = split_heads(key_in, head_dim)
    value_three = split_heads(value_in, head_dim)
    has_first = first != my_dev
    prev_index = jnp.maximum(my_dev - 1, 0)
    prev_used = (my_dev > 0) & (group_mask[my_dev, prev_index] == 1) & (first != my_dev - 1)
    shared = from_root(jnp.stack([key_in, value_in]), "tm", first)
    first_keys = split_heads(shared[0], head_dim)
    first_values = split_heads(shared[1], head_dim)
    blank = empty_stats(heads_loc, rows_loc)
    zero_three = jnp.zeros((rows_loc, heads_loc, head_dim), jnp.float32)
    zero_grads = (zero_three, zero_three, zero_three)
    diag_stats = pair_stats(query_three, grad_three, key_three, value_three, scale)
    first_stats = lax.cond(
        has_first,
        lambda: pair_stats(query_three, grad_three, first_keys, first_values, scale),
        lambda: blank,
    )
    running = merge_stats(diag_stats, first_stats)
    prev_pair = passed_along(jnp.stack([key_in, value_in]), "tm", 1)
    prev_keys = split_heads(prev_pair[0], head_dim)
    prev_values = split_heads(prev_pair[1], head_dim)
    prev_stats = lax.cond(
        prev_used,
        lambda: pair_stats(query_three, grad_three, prev_keys, prev_values, scale),
        lambda: blank,
    )
    row_max, row_sum, row_dot = merge_stats(running, prev_stats)
    log_sums = row_max + jnp.log(row_sum)
    deltas = row_dot / row_sum
    query_acc, key_acc, value_acc = pair_grads(
        query_three, grad_three, log_sums, deltas, key_three, value_three, scale
    )
    first_query, first_key, first_value = lax.cond(
        has_first,
        lambda: pair_grads(
            query_three, grad_three, log_sums, deltas, first_keys, first_values, scale
        ),
        lambda: zero_grads,
    )
    query_acc = query_acc + first_query
    prev_query_term, prev_key_term, prev_value_term = lax.cond(
        prev_used,
        lambda: pair_grads(
            query_three, grad_three, log_sums, deltas, prev_keys, prev_values, scale
        ),
        lambda: zero_grads,
    )
    query_acc = query_acc + prev_query_term
    returned = passed_along(
        jnp.stack([prev_key_term, prev_value_term]).astype(jnp.bfloat16), "tm", -1
    ).astype(jnp.float32)
    key_acc = key_acc + returned[0]
    value_acc = value_acc + returned[1]
    key_total, value_total = (
        lax.psum(first_key.astype(jnp.bfloat16), "tm").astype(jnp.float32),
        lax.psum(first_value.astype(jnp.bfloat16), "tm").astype(jnp.float32),
    )
    is_owner = my_dev == first
    key_acc = key_acc + jnp.where(is_owner, key_total, 0.0)
    value_acc = value_acc + jnp.where(is_owner, value_total, 0.0)
    query_out = query_acc.reshape(rows_loc, width_loc).astype(jnp.bfloat16)
    key_out = key_acc.reshape(rows_loc, width_loc).astype(jnp.bfloat16)
    value_out = value_acc.reshape(rows_loc, width_loc).astype(jnp.bfloat16)
    return (query_out, key_out, value_out)


def solution(mesh):
    placed = (
        P("tm", "head"),
        P("tm", "head"),
        P("tm", "head"),
        P("tm", "head"),
        P("head", None),
        P(),
        P(),
    )
    return jax.shard_map(
        local,
        mesh=mesh,
        in_specs=placed,
        out_specs=(P("tm", "head"), P("tm", "head"), P("tm", "head")),
        check_vma=False,
    )
```

profile of v0, /device:TPU:0, one launch (start us, length us, event | category | flops | bytes accessed | tf_op | source)
XLA Modules:
  0.0 411.6 jit_solution(18054340109988929187)
XLA Ops:
  8.7 3.8 broadcast_select_fusion
  13.2 5.2 %collective-permute-start = (bf16[2,784,640]{2,1,0:T(8,128)(2,1)}, bf16[2,784,640]{2,1,0:T(8,128)(2,1)}, u32[]{:S(2)}, u32[]{:S(2)}) collective-permute-start(bf16[2,784,640]{2,1,0:T(8,128)(2,1)} %get-tuple-element.145), channel_id=1, source_target_pairs={{0,8},{8,16},{16,24},{24,32},{32,40},{40,48},{48,56},{56,64},{64,7... | collective-permute-start | bytes 6021128 | tf_op jit(solution)/shard_map/ppermute | solution.py:20
  23.1 2.0 copy.28
  25.1 7.6 %multiply_reduce_fusion.5 = (f32[5,784]{1,0:T(8,128)S(1)}, f32[5,784,784]{1,2,0:T(8,128)}) fusion(bf16[784,5,128]{0,2,1:T(8,128)(2,1)S(1)} %bitcast.97, bf16[784,5,128]{0,2,1:T(8,128)(2,1)S(1)} %bitcast.113), kind=kOutput, calls=%fused_computation.36 | convolution fusion | flops 792902336 | bytes 14315840 | tf_op jit(solution)/shard_map/qhd,khd->hqk/dot_general | solution.py:53
  32.7 104.3 %all-reduce.4.cloned.1.call-done = bf16[2,784,640]{2,1,0:T(8,128)(2,1)} async-done(((bf16[2,784,640]{2,1,0:T(8,128)(2,1)}), bf16[2,784,640]{2,1,0:T(8,128)(2,1)}) %all-reduce.4.cloned.1.call-update) | async-done | bytes 2007056 | tf_op jit(solution)/shard_map/psum | solution.py:14
  141.5 2.6 fusion.42
  144.1 2.4 copy.40
  148.2 11.5 %convolution_convert_fusion = bf16[784,640]{1,0:T(8,128)(2,1)} fusion(bf16[784,5120]{1,0:T(8,128)(2,1)} %all-gather.2.cloned.1.call-done, bf16[640,5120]{1,0:T(8,128)(2,1)} %param.19), kind=kOutput, calls=%fused_computation.54 | convolution fusion | flops 5138524160 | bytes 15585280 | tf_op jit(solution)/shard_map/dot_general | solution.py:77
  161.7 20.0 %conditional.4 = (f32[5,784]{1,0:T(8,128)}, f32[5,784]{1,0:T(8,128)S(1)}, f32[5,784]{1,0:T(8,128)S(1)}) conditional(s32[]{:T(128)} %convert_element_type.63, () %tuple.44, (bf16[784,5,128]{0,2,1:T(8,128)(2,1)S(1)}, bf16[784,5,128]{0,2,1:T(8,128)(2,1)S(1)}, bf16[784,5,128]{0,2,1:T(8,128)(2,1)S(1)}, bf16[784,5,128]{0,2,1:T(8,128)(2,1)}) %tuple.102), branch_computations={%region_2.3_spmd, %region_3.7_spmd} | conditional | flops 1601167104 | bytes 94158480 | solution.py:97
  162.2 2.6 multiply_reduce_fusion.1
  164.8 5.1 %copy-done = f32[5,784,784]{1,2,0:T(8,128)} copy-done((f32[5,784,784]{1,2,0:T(8,128)}, f32[5,784,784]{1,2,0:T(8,128)S(1)}, u32[]{:S(2)}) %copy-start) | copy-done | bytes 12293144 | tf_op jit(solution)/shard_map/cond
  169.9 4.4 %multiply_reduce_fusion = f32[5,784]{1,0:T(8,128)S(1)} fusion(f32[5,784,784]{1,2,0:T(8,128)S(1)} %get-tuple-element.139, bf16[784,5,128]{0,2,1:T(8,128)(2,1)S(1)} %get-tuple-element.113, bf16[784,5,128]{0,2,1:T(8,128)(2,1)S(1)} %copy-done.9, f32[5,784]{1,0:T(8,128)} %get-tuple-element.162), kind=kOutput, calls=%fused_computation | convolution fusion | flops 799048896 | bytes 14331520 | tf_op jit(solution)/shard_map/cond/branch_1_fun/qhd,khd->hqk/dot_general | solution.py:41
  174.3 7.4 %fusion = f32[5,784]{1,0:T(8,128)S(1)} fusion(f32[5,784,784]{1,2,0:T(8,128)} %copy-done, f32[5,784]{1,0:T(8,128)} %get-tuple-element.162), kind=kLoop, calls=%fused_computation.3 | loop fusion | flops 9215920 | bytes 12324480 | tf_op jit(solution)/shard_map/cond/branch_1_fun/reduce_sum | solution.py:42
  183.1 11.5 %multiply_reduce_fusion.4 = (f32[5,784]{1,0:T(8,128)S(1)}, f32[5,784]{1,0:T(8,128)S(1)}, f32[5,784,784]{1,2,0:T(8,128)}) fusion(f32[5,784,784]{1,2,0:T(8,128)} %get-tuple-element.151, f32[5,784]{1,0:T(8,128)S(1)} %get-tuple-element.150, bf16[784,5,128]{0,2,1:T(8,128)(2,1)S(1)} %bitcast.105, bf16[784,5,128]{0,2,1:T(8,128)(2,1)} %bitcast.122), kind=kOutput, calls=%fused_computation.31 | convolution fusion | flops 802118272 | bytes 26640320 | tf_op jit(solution)/shard_map/qhd,khd->hqk/dot_general | solution.py:59
  195.5 13.9 %conditional.7 = (f32[784,5,128]{2,0,1:T(8,128)}, bf16[1,784,5,128]{3,1,2,0:T(8,128)(2,1)}, bf16[1,784,5,128]{3,1,2,0:T(8,128)(2,1)}) conditional(s32[]{:T(128)} %convert_element_type.65, () %tuple.50, (bf16[784,5,128]{0,2,1:T(8,128)(2,1)S(1)}, bf16[784,5,128]{0,2,1:T(8,128)(2,1)S(1)}, f32[5,784]{1,0:T(8,128)S(1)}, ...), branch_computations={%region_16.17_spmd, %region_17.18_spmd} | conditional | flops 3960391680 | bytes 74433040 | solution.py:125
  209.4 3.0 pad_maximum_fusion.1
  213.7 33.6 %conditional.6 = (f32[784,5,128]{2,0,1:T(8,128)}, f32[784,5,128]{2,0,1:T(8,128)}, f32[784,5,128]{2,0,1:T(8,128)}) conditional(s32[]{:T(128)} %convert_element_type.63, () %tuple.48, (bf16[784,5,128]{0,2,1:T(8,128)(2,1)S(1)}, bf16[784,5,128]{0,2,1:T(8,128)(2,1)S(1)}, f32[5,784]{1,0:T(8,128)S(1)}, bf16[784,5,128]{0,2,1:T(8,128)(2,1)S(1)}, ...), branch_computations={%region_14.15_spmd, %region_15.16_spmd} | conditional | flops 3959388160 | bytes 68411864 | solution.py:117
  213.7 7.0 %fusion.43 = f32[5,784,784]{2,1,0:T(8,128)} fusion(bf16[784,5,128]{0,2,1:T(8,128)(2,1)S(1)} %get-tuple-element.119, bf16[784,5,128]{0,2,1:T(8,128)(2,1)S(1)} %get-tuple-element.120), kind=kOutput, calls=%fused_computation.65 | convolution fusion | flops 786759680 | bytes 14300160 | tf_op jit(solution)/shard_map/cond/branch_1_fun/qhd,khd->hqk/dot_general | solution.py:53
  220.7 10.1 %fusion.7 = f32[784,5,128]{2,0,1:T(8,128)} fusion(bf16[784,5,128]{0,2,1:T(8,128)(2,1)S(1)} %get-tuple-element.122, f32[5,784,784]{2,1,0:T(8,128)} %fusion.43, f32[5,784]{1,0:T(8,128)S(1)} %get-tuple-element.52), kind=kOutput, calls=%fused_computation.16 | convolution fusion | flops 795979520 | bytes 15319360 | tf_op jit(solution)/shard_map/cond/branch_1_fun/hqk,qhd->khd/dot_general | solution.py:58
  230.7 9.1 %multiply_convert_fusion = bf16[5,784,784]{2,1,0:T(8,128)(2,1)S(1)} fusion(f32[5,784,784]{2,1,0:T(8,128)} %fusion.43, bf16[784,5,128]{0,2,1:T(8,128)(2,1)S(1)} %get-tuple-element.122, bf16[784,5,128]{0,2,1:T(8,128)(2,1)} %get-tuple-element.123, f32[5,784]{1,0:T(8,128)S(1)} %get-tuple-element.55, f32[5,784]{1,0:T(8,128)S(1)} %get-tuple-element.52), kind=kOutput, calls=%fused_computation.8 | convolution fusion | flops 802126080 | bytes 20478080 | tf_op jit(solution)/shard_map/cond/branch_1_fun/qhd,khd->hqk/dot_general | solution.py:59
  239.9 3.9 multiply_bitcast_fusion
  243.7 3.4 multiply_bitcast_fusion.1
  247.3 2.6 convert_element_type.70
  250.0 2.6 convert_element_type.75
  252.7 10.2 %multiply_convert_fusion.3 = bf16[5,784,784]{1,2,0:T(8,128)(2,1)S(1)} fusion(f32[5,784,784]{1,2,0:T(8,128)} %get-tuple-element.152, f32[5,784,784]{1,2,0:T(8,128)} %get-tuple-element.151, f32[5,784]{1,0:T(8,128)S(1)} %get-tuple-element.148, f32[5,784]{1,0:T(8,128)S(1)} %get-tuple-element.149), kind=kLoop, calls=%fused_computation.30 | loop fusion | flops 15366400 | bytes 30764160 | tf_op jit(solution)/shard_map/convert_element_type | solution.py:60
  262.9 2.8 copy-done.2
  265.6 5.8 %fusion.37 = bf16[784,5,128]{2,0,1:T(8,128)(2,1)} fusion(f32[784,5,128]{2,0,1:T(8,128)} %get-tuple-element.84, f32[784,5,128]{2,0,1:T(8,128)} %get-tuple-element.83, bf16[5,784,784]{1,2,0:T(8,128)(2,1)S(1)} %multiply_convert_fusion.3, bf16[784,5,128]{0,2,1:T(8,128)(2,1)S(1)} %bitcast.114), kind=kOutput, calls=%fused_computation.52 | convolution fusion | flops 788766720 | bytes 12167680 | tf_op jit(solution)/shard_map/hqk,khd->qhd/dot_general | solution.py:61
  271.4 2.0 copy.58
  275.1 3.7 convert_element_type.69
  278.8 105.2 %all-reduce.6.cloned.1.call-done = (bf16[784,5,128]{2,0,1:T(8,128)(2,1)}, bf16[784,5,128]{2,0,1:T(8,128)(2,1)}) async-done(((bf16[784,5,128]{2,0,1:T(8,128)(2,1)}, bf16[784,5,128]{2,0,1:T(8,128)(2,1)}), (bf16[784,5,128]{2,0,1:T(8,128)(2,1)}, bf16[784,5,128]{2,0,1:T(8,128)(2,1)})) %all-reduce.6.cloned.1.call-update) | async-done | bytes 2007056 | tf_op jit(solution)/shard_map/psum | solution.py:139
  384.1 8.7 %fusion.32 = bf16[784,5,128]{2,0,1:T(8,128)(2,1)S(1)} fusion(f32[2,784,5,128]{3,1,2,0:T(8,128)} %convert_element_type.69, bf16[784,5,128]{2,0,1:T(8,128)(2,1)} %get-tuple-element.137, bf16[784,5,128]{0,2,1:T(8,128)(2,1)S(1)} %bitcast.108, f32[5,784,784]{1,2,0:T(8,128)} %get-tuple-element.151, f32[5,784]{1,0:T(8,128)S(1)} %get-tuple-element.149, pred[]{:T(512)S(6)} %eq.10), kind=kOutput, calls=%fused_computation.43 | convolution fusion | flops 798488320 | bytes 17326400 | tf_op jit(solution)/shard_map/hqk,qhd->khd/dot_general | solution.py:58
  392.8 5.1 %fusion.35 = bf16[784,5,128]{2,0,1:T(8,128)(2,1)S(1)} fusion(f32[2,784,5,128]{3,1,2,0:T(8,128)S(1)} %copy-done.8, bf16[784,5,128]{2,0,1:T(8,128)(2,1)S(1)} %copy-done.16, bf16[5,784,784]{1,2,0:T(8,128)(2,1)} %copy-done.2, bf16[784,5,128]{0,2,1:T(8,128)(2,1)S(1)} %bitcast.102, pred[]{:T(512)S(6)} %eq.10), kind=kOutput, calls=%fused_computation.47 | convolution fusion | flops 789770240 | bytes 11164161 | tf_op jit(solution)/shard_map/hqk,qhd->khd/dot_general | solution.py:64
  (55 shorter events, 28.2 us)
Async XLA Ops:
  8.0 129.1 %all-reduce.4.cloned.1.call-start = ((), (), s32[]{:S(2)}) async-start(), calls=%async_computation | async-start | bytes 4014080 | tf_op jit(solution)/shard_map/psum | solution.py:14
  12.5 5.9 %copy-start.11 = (bf16[784,640]{1,0:T(8,128)(2,1)S(1)}, bf16[784,640]{1,0:T(8,128)(2,1)}, u32[]{:S(2)}) copy-start(bf16[784,640]{1,0:T(8,128)(2,1)} %param.16) | copy-start | bytes 3010564
  12.6 6.9 %copy-start.12 = (bf16[784,640]{1,0:T(8,128)(2,1)S(1)}, bf16[784,640]{1,0:T(8,128)(2,1)}, u32[]{:S(2)}) copy-start(bf16[784,640]{1,0:T(8,128)(2,1)} %param.17) | copy-start | bytes 3010564
  12.6 135.6 %all-gather.2.cloned.1.call-start = ((), (), s32[]{:S(2)}) async-start(), calls=%async_computation.1 | async-start | bytes 9031680 | tf_op jit(solution)/shard_map/all_gather | solution.py:78
  13.2 370.9 %all-reduce.6.cloned.1.call-start = ((), (), s32[]{:S(2)}) async-start(), calls=%async_computation.2 | async-start | bytes 4014080 | tf_op jit(solution)/shard_map/psum | solution.py:139
  13.2 128.3 %collective-permute-start = (bf16[2,784,640]{2,1,0:T(8,128)(2,1)}, bf16[2,784,640]{2,1,0:T(8,128)(2,1)}, u32[]{:S(2)}, u32[]{:S(2)}) collective-permute-start(bf16[2,784,640]{2,1,0:T(8,128)(2,1)} %get-tuple-element.145), channel_id=1, source_target_pairs={{0,8},{8,16},{16,24},{24,32},{32,40},{40,48},{48,56},{56,64},{64,7... | collective-permute-start | bytes 6021128 | tf_op jit(solution)/shard_map/ppermute | solution.py:20
  19.5 5.6 %copy-start.6 = (bf16[784,640]{0,1:T(8,128)(2,1)}, bf16[784,640]{0,1:T(8,128)(2,1)S(1)}, u32[]{:S(2)}) copy-start(bf16[784,640]{0,1:T(8,128)(2,1)S(1)} %copy.29) | copy-start | bytes 3010564
  162.2 7.8 %copy-start.9 = (bf16[784,5,128]{0,2,1:T(8,128)(2,1)S(1)}, bf16[784,5,128]{0,2,1:T(8,128)(2,1)}, u32[]{:S(2)}) copy-start(bf16[784,5,128]{0,2,1:T(8,128)(2,1)} %get-tuple-element.114) | copy-start | bytes 3010564 | tf_op jit(solution)/shard_map/cond
  164.8 5.1 %copy-start = (f32[5,784,784]{1,2,0:T(8,128)}, f32[5,784,784]{1,2,0:T(8,128)S(1)}, u32[]{:S(2)}) copy-start(f32[5,784,784]{1,2,0:T(8,128)S(1)} %get-tuple-element.139) | copy-start | bytes 36879364 | tf_op jit(solution)/shard_map/cond
  181.7 0.6 copy-start.13
  183.1 11.6 %copy-start.15 = (f32[5,784]{1,0:T(8,128)}, f32[5,784]{1,0:T(8,128)S(1)}, u32[]{:S(2)}) copy-start(f32[5,784]{1,0:T(8,128)S(1)} %get-tuple-element.82) | copy-start | bytes 47044
  183.1 11.6 %copy-start.14 = (f32[5,784]{1,0:T(8,128)S(1)}, f32[5,784]{1,0:T(8,128)}, u32[]{:S(2)}) copy-start(f32[5,784]{1,0:T(8,128)} %copy-done.13) | copy-start | bytes 47044
  183.1 12.4 %copy-start.3 = (bf16[1,784,640]{1,2,0:T(8,128)(2,1)S(1)}, bf16[1,784,640]{1,2,0:T(8,128)(2,1)}, u32[]{:S(2)}) copy-start(bf16[1,784,640]{1,2,0:T(8,128)(2,1)} %copy.39) | copy-start | bytes 3010564
  212.4 62.7 %collective-permute-start.1 = (bf16[2,784,5,128]{3,1,2,0:T(8,128)(2,1)}, bf16[2,784,5,128]{3,1,2,0:T(8,128)(2,1)}, u32[]{:S(2)}, u32[]{:S(2)}) collective-permute-start(bf16[2,784,5,128]{3,1,2,0:T(8,128)(2,1)} %pad_maximum_fusion.1), channel_id=1, source_target_pairs={{8,0},{16,8},{24,16},{32,24},{40,32},{48,40},{56,48},{64,56},{72,6... | collective-permute-start | bytes 6021128 | tf_op jit(solution)/shard_map/ppermute | solution.py:20
  252.6 13.0 %copy-start.7 = (bf16[784,640]{0,1:T(8,128)(2,1)S(1)}, bf16[784,640]{0,1:T(8,128)(2,1)}, u32[]{:S(2)}) copy-start(bf16[784,640]{0,1:T(8,128)(2,1)} %copy-done.6) | copy-start | bytes 3010564
  262.9 2.8 copy-start.2
  384.0 8.7 %copy-start.8 = (f32[2,784,5,128]{3,1,2,0:T(8,128)S(1)}, f32[2,784,5,128]{3,1,2,0:T(8,128)}, u32[]{:S(2)}) copy-start(f32[2,784,5,128]{3,1,2,0:T(8,128)} %convert_element_type.69) | copy-start | bytes 12042244
  384.1 8.7 %copy-start.16 = (bf16[784,5,128]{2,0,1:T(8,128)(2,1)S(1)}, bf16[784,5,128]{2,0,1:T(8,128)(2,1)}, u32[]{:S(2)}) copy-start(bf16[784,5,128]{2,0,1:T(8,128)(2,1)} %get-tuple-element.136) | copy-start | bytes 3010564
Sparse Core Ops, SparseCore 0:
  12.7 124.3 all-reduce.3
  252.8 131.2 all-reduce.5
Sparse Core Ops, SparseCore 1:
  14.7 50.4 all-gather.1
where the time goes:
time: 419 us; the launch traced here: 412 us
  waiting for transfers between devices  210 us (50%)
  matrix products  90.6 us (22%)
  local copies, waits for them, and re-layouts  41.6 us (10%)
  other arithmetic  34.2 us (8%)
  between operations  17.3 us (4%)
  loops' own time  11.2 us (3%)
  starting transfers between devices  6.6 us (2%)
    psum x1, waiting for transfers between devices, local(): lax.psum(first_key.astype(jnp.bfloat16), 'tm').astype(jnp.float32)  105 us
    psum x1, waiting for transfers between devices, from_root(): return lax.psum(jnp.where(mine, shard, jnp.zeros_like(shard)), axis)  104 us
    dot_general x2, matrix products, pair_grads(): jnp.einsum('qhd,khd->hqk', grad_blk, value_blk, preferred_element_type=jn...  20.6 us
    dot_general x2, matrix products, pair_grads(): jnp.einsum('hqk,qhd->khd', probs_low, grad_blk, preferred_element_type=jn...  18.7 us
    dot_general x2, matrix products, pair_grads(): jnp.einsum('qhd,khd->hqk', query_blk, key_blk, preferred_element_type=jnp...  14.6 us
    unnamed x28, local copies, waits for them, and re-layouts  13.2 us
    dot_general x1, matrix products, local(): lax.dot_general(lax.all_gather(layer_grad, 'head', axis=1, tiled=True), o...  11.5 us
    another operation x1, loops' own time, local(): lax.cond(prev_used, lambda: pair_grads(query_three, grad_three, log_sums,...  10.4 us
  transfers between devices with their start and end apart: 5, of which 2 were waited for; matrix products, arithmetic and copies ran while one was open for 21% of the time, Pallas kernels for 0%

commit v1 on v0

v1 whole, which is shorter than its diff:
```python
import functools
import math

import jax
import jax.numpy as jnp
from jax import lax
from jax.experimental import pallas as pl
from jax.experimental.pallas import tpu as pltpu
from jax.sharding import PartitionSpec as P

MESH = pl.DeviceIdType.MESH
D_HEAD = 128
SIDE = 4
CHUNK = 224
LAG = 2
SLOTS = 4
ROW_CUT = 400
VMEM_LIMIT = 60 * 1024 * 1024
LOWEST = -1e30
NT = (((1,), (1,)), ((), ()))
NN = (((1,), (0,)), ((), ()))
TN = (((0,), (0,)), ((), ()))


class Place:
    def __init__(self):
        tm, head = lax.axis_index("tm"), lax.axis_index("head")
        self.tm, self.head = tm, head
        x, z = tm // SIDE, tm % SIDE
        self.x, self.z = x, z
        self.sib_head = head + 1 - 2 * (head % 2)
        self.up_head = (head + 2) % 8
        self.down_head = (head + 6) % 8
        self.far_head = (head + 4) % 8
        self.sib = (tm, self.sib_head)
        self.up = (tm, self.up_head)
        self.down = (tm, self.down_head)
        self.after = ((tm + 1) % 16, head)
        self.before = ((tm + 15) % 16, head)
        self.zup = (x * SIDE + (z + 1) % SIDE, head)
        self.zdown = (x * SIDE + (z + 3) % SIDE, head)
        self.xup = (((x + 1) % SIDE) * SIDE + z, head)
        self.xdown = (((x + 3) % SIDE) * SIDE + z, head)


def meet(peers):
    barrier = pltpu.get_barrier_semaphore()
    for peer in peers:
        pl.semaphore_signal(barrier, inc=1, device_id=peer, device_id_type=MESH)
    pl.semaphore_wait(barrier, len(peers))


def remote(src, dst, send, recv, peer):
    return pltpu.make_async_remote_copy(
        src_ref=src, dst_ref=dst, send_sem=send, recv_sem=recv, device_id=peer, device_id_type=MESH
    )


def chunk_of(ref, c, per_head):
    rows = pl.ds(pl.multiple_of((c % per_head) * CHUNK, CHUNK), CHUNK)
    cols = pl.ds(pl.multiple_of((c // per_head) * D_HEAD, D_HEAD), D_HEAD)
    return ref.at[rows, cols]


class Chain:
    def __init__(self, slots, stage, send, recv, peer, chunks):
        self.slots, self.stage, self.send, self.recv = slots, stage, send, recv
        self.peer, self.chunks = peer, chunks
        self.steps = chunks + 2 * LAG

    def copy(self, t):
        s = lax.rem(t, SLOTS)
        return remote(
            self.stage.at[s], self.slots.at[t], self.send.at[s], self.recv.at[t], self.peer
        )

    def step(self, t, fill):
        @pl.when((t >= LAG) & (t < self.steps + LAG))
        def _():
            self.copy(t - LAG).wait_recv()

        @pl.when((t >= 0) & (t < self.steps))
        def _():
            @pl.when(t >= SLOTS)
            def _():
                self.copy(t - SLOTS).wait_send()

            fill(t, self.stage.at[lax.rem(t, SLOTS)])
            self.copy(t).start()

    def drain(self):
        def one(t, carry):
            self.copy(t).wait_send()
            return carry

        lax.fori_loop(self.steps - SLOTS, self.steps, one, 0)


def spread_fill(chain, own, per_head, at_root):
    def fill(t, stage):
        mine = chunk_of(own, jnp.minimum(t, chain.chunks - 1), per_head)

        @pl.when(t < LAG)
        def _():
            stage[...] = mine[...]

        @pl.when(t >= LAG)
        def _():
            stage[...] = lax.select(at_root, mine[...], chain.slots[t - LAG])

    return fill


def spread_result(chain, u, own, hops):
    near = lax.select(hops == 0, own, chain.slots[u])
    far = lax.select(hops == 2, chain.slots[u + LAG], chain.slots[u + 2 * LAG])
    return lax.select(hops < 2, near, far)


def gather_kernel(
    first_ref, g_hbm, w_hbm, k_hbm, v_hbm,
    do_ref, shared_ref, prev_ref,
    gathered, weight, total, kv,
    slots_x, slots_z, stage_x, stage_z,
    load_sem, side_send, side_recv, up_send, up_recv, down_send, down_recv,
    prev_send, prev_recv, x_send, x_recv, z_send, z_recv,
):
    at = Place()
    rows, width = do_ref.shape
    per_head = 2 * rows // CHUNK
    chunks = per_head * (width // D_HEAD)
    loads = [
        pltpu.make_async_copy(g_hbm, gathered.at[at.head], load_sem.at[0]),
        pltpu.make_async_copy(k_hbm, kv.at[pl.ds(0, rows)], load_sem.at[1]),
        pltpu.make_async_copy(v_hbm, kv.at[pl.ds(rows, rows)], load_sem.at[2]),
        pltpu.make_async_copy(w_hbm, weight, load_sem.at[3]),
    ]
    for load in loads:
        load.start()
    meet([at.sib, at.up, at.down, at.after, at.before, at.zup, at.zdown, at.xup, at.xdown])

    top, low = pl.ds(0, ROW_CUT), pl.ds(ROW_CUT, rows - ROW_CUT)

    def half(head, part):
        return gathered.at[head, part]

    def send(head, part, sems, n, peer):
        return remote(half(head, part), half(head, part), sems[0].at[n], sems[1].at[n], peer)

    side, up, down = (side_send, side_recv), (up_send, up_recv), (down_send, down_recv)
    loads[0].wait()
    started = []

    def go(*args):
        copy = send(*args)
        copy.start()
        started.append(copy)

    go(at.head, top, up, 0, at.up)
    go(at.head, low, down, 0, at.down)
    go(at.head, low, up, 1, at.up)
    go(at.head, top, down, 1, at.down)
    go(at.head, pl.ds(0, rows), side, 0, at.sib)
    prevs = [
        remote(k_hbm, prev_ref.at[0], prev_send.at[0], prev_recv.at[0], at.after),
        remote(v_hbm, prev_ref.at[1], prev_send.at[1], prev_recv.at[1], at.after),
    ]
    for copy in prevs:
        copy.start()
    loads[1].wait()
    loads[2].wait()

    first = first_ref[0]
    hops_x = (first // SIDE - at.x) & (SIDE - 1)
    hops_z = (first % SIDE - at.z) & (SIDE - 1)
    chain_x = Chain(slots_x, stage_x, x_send, x_recv, at.xdown, chunks)
    chain_z = Chain(slots_z, stage_z, z_send, z_recv, at.zdown, chunks)
    fill_x = spread_fill(chain_x, kv, per_head, hops_x == 0)
    fill_z = spread_fill(chain_z, shared_ref, per_head, hops_z == 0)

    def chain_step(t, carry):
        chain_x.step(t, fill_x)
        u = t - 3 * LAG

        @pl.when((u >= 0) & (u < chunks))
        def _():
            mine = chunk_of(kv, u, per_head)[...]
            chunk_of(shared_ref, u, per_head)[...] = spread_result(chain_x, u, mine, hops_x)

        chain_z.step(u, fill_z)
        w = u - 3 * LAG

        @pl.when(w >= 0)
        def _():
            mine = chunk_of(shared_ref, w, per_head)
            mine[...] = spread_result(chain_z, w, mine[...], hops_z)

        return carry

    def project(head, fresh=False):
        cols = pl.ds(pl.multiple_of(head * width, width), width)
        part = lax.dot_general(
            gathered[head], weight[:, cols], NT, preferred_element_type=jnp.float32
        )
        total[...] = part if fresh else total[...] + part

    end = chunks + 6 * LAG
    lax.fori_loop(0, 3, chain_step, 0)
    loads[3].wait()
    project(at.head, fresh=True)
    lax.fori_loop(3, 5, chain_step, 0)
    send(at.sib_head, pl.ds(0, rows), side, 0, at.sib).wait_recv()
    project(at.sib_head)
    lax.fori_loop(5, 9, chain_step, 0)
    send(at.down_head, top, up, 0, at.up).wait_recv()
    go(at.down_head, top, up, 2, at.up)
    go(at.down_head, top, side, 1, at.sib)
    send(at.up_head, low, down, 0, at.down).wait_recv()
    go(at.up_head, low, down, 2, at.down)
    go(at.up_head, low, side, 2, at.sib)
    lax.fori_loop(9, 18, chain_step, 0)
    send(at.down_head, low, up, 1, at.up).wait_recv()
    go(at.down_head, low, side, 3, at.sib)
    send(at.up_head, top, down, 1, at.down).wait_recv()
    go(at.up_head, top, side, 4, at.sib)
    project(at.down_head)
    lax.fori_loop(18, 19, chain_step, 0)
    project(at.up_head)
    lax.fori_loop(19, 21, chain_step, 0)
    down_sib, up_sib, far_sib = [h + 1 - 2 * (h % 2) for h in (at.down_head, at.up_head, at.far_head)]
    send(down_sib, top, side, 1, at.sib).wait_recv()
    send(down_sib, low, side, 3, at.sib).wait_recv()
    project(down_sib)
    lax.fori_loop(21, 22, chain_step, 0)
    send(up_sib, low, side, 2, at.sib).wait_recv()
    send(up_sib, top, side, 4, at.sib).wait_recv()
    project(up_sib)
    lax.fori_loop(22, 27, chain_step, 0)
    send(at.far_head, top, up, 2, at.up).wait_recv()
    go(at.far_head, top, side, 5, at.sib)
    send(at.far_head, low, down, 2, at.down).wait_recv()
    go(at.far_head, low, side, 6, at.sib)
    project(at.far_head)
    lax.fori_loop(27, 29, chain_step, 0)
    send(far_sib, top, side, 5, at.sib).wait_recv()
    send(far_sib, low, side, 6, at.sib).wait_recv()
    project(far_sib)
    do_ref[...] = total[...].astype(do_ref.dtype)
    lax.fori_loop(29, end, chain_step, 0)
    for copy in prevs:
        copy.wait_recv()
        copy.wait_send()
    for copy in started:
        copy.wait_send()
    chain_x.drain()
    chain_z.drain()


def gather(first_group, g, w, k, v):
    rows, width = g.shape
    chunks = (2 * rows // CHUNK) * (width // D_HEAD)
    steps = chunks + 2 * LAG
    bf = jnp.bfloat16
    dma = pltpu.SemaphoreType.DMA
    anywhere = pl.BlockSpec(memory_space=pl.ANY)
    vmem = pl.BlockSpec(memory_space=pltpu.VMEM)
    return pl.pallas_call(
        gather_kernel,
        out_shape=[
            jax.ShapeDtypeStruct((rows, width), bf),
            jax.ShapeDtypeStruct((2 * rows, width), bf),
            jax.ShapeDtypeStruct((2, rows, width), bf),
        ],
        in_specs=[pl.BlockSpec(memory_space=pltpu.SMEM)] + [anywhere] * 4,
        out_specs=[vmem, vmem, anywhere],
        scratch_shapes=[
            pltpu.VMEM((8, rows, width), bf),
            pltpu.VMEM(w.shape, bf),
            pltpu.VMEM((rows, width), jnp.float32),
            pltpu.VMEM((2 * rows, width), bf),
            pltpu.VMEM((steps, CHUNK, D_HEAD), bf),
            pltpu.VMEM((steps, CHUNK, D_HEAD), bf),
            pltpu.VMEM((SLOTS, CHUNK, D_HEAD), bf),
            pltpu.VMEM((SLOTS, CHUNK, D_HEAD), bf),
            dma((4,)),
            dma((7,)), dma((7,)), dma((3,)), dma((3,)), dma((3,)), dma((3,)),
            dma((2,)), dma((2,)),
            dma((SLOTS,)), dma((steps,)), dma((SLOTS,)), dma((steps,)),
        ],
        compiler_params=pltpu.CompilerParams(
            collective_id=0, has_side_effects=True, vmem_limit_bytes=VMEM_LIMIT
        ),
        name="gather",
    )(first_group, g, w, k, v)


def attend_kernel(
    bias_ref, q_ref, k_ref, v_ref, do_ref, shared_ref, prev_ref,
    dq_ref, own_ref, first_ref, back_ref,
    keys, values, scores, dprobs, probs_low, ds_low,
):
    rows, width = q_ref.shape
    scale = D_HEAD ** (-0.5)
    step = 112
    blocks = rows // step

    def head_body(h, carry):
        cols = pl.ds(pl.multiple_of(h * D_HEAD, D_HEAD), D_HEAD)
        keys[0:rows] = k_ref[:, cols]
        values[0:rows] = v_ref[:, cols]
        keys[rows : 2 * rows] = shared_ref[0:rows, cols]
        values[rows : 2 * rows] = shared_ref[rows : 2 * rows, cols]
        keys[2 * rows : 3 * rows] = prev_ref[0, :, cols]
        values[2 * rows : 3 * rows] = prev_ref[1, :, cols]
        q, do = q_ref[:, cols], do_ref[:, cols]

        def score_block(i, peak):
            part = pl.ds(pl.multiple_of(i * step, step), step)
            s = lax.dot_general(keys[part], q, NT, preferred_element_type=jnp.float32)
            s = s * (scale * math.log2(math.e)) + bias_ref[i // blocks]
            scores[part] = s
            return jnp.maximum(peak, jnp.max(s, axis=0, keepdims=True))

        peak = lax.fori_loop(
            0, 3 * blocks, score_block, jnp.full((1, rows), 2 * LOWEST, jnp.float32)
        )

        def weight_block(i, sums):
            part = pl.ds(pl.multiple_of(i * step, step), step)
            dp = lax.dot_general(values[part], do, NT, preferred_element_type=jnp.float32)
            e = jnp.exp2(scores[part] - peak)
            scores[part] = e
            dprobs[part] = dp
            return (
                sums[0] + jnp.sum(e, axis=0, keepdims=True),
                sums[1] + jnp.sum(e * dp, axis=0, keepdims=True),
            )

        zero = jnp.zeros((1, rows), jnp.float32)
        mass, dot = lax.fori_loop(0, 3 * blocks, weight_block, (zero, zero))
        inverse = 1.0 / mass
        delta = dot * inverse

        def grad_block(i, carry):
            part = pl.ds(pl.multiple_of(i * step, step), step)
            p = scores[part] * inverse
            probs_low[part] = p.astype(jnp.bfloat16)
            ds_low[part] = (p * (dprobs[part] - delta)).astype(jnp.bfloat16)
            return carry

        lax.fori_loop(0, 3 * blocks, grad_block, 0)
        for pair, out in enumerate((own_ref, first_ref, back_ref)):
            part = pl.ds(pair * rows, rows)
            dv = lax.dot_general(probs_low[part], do, NN, preferred_element_type=jnp.float32)
            dk = lax.dot_general(ds_low[part], q, NN, preferred_element_type=jnp.float32)
            out[0:rows, cols] = (dk * scale).astype(jnp.bfloat16)
            out[rows : 2 * rows, cols] = dv.astype(jnp.bfloat16)
        dq = lax.dot_general(ds_low[...], keys[...], TN, preferred_element_type=jnp.float32)
        dq_ref[:, cols] = (dq * scale).astype(jnp.bfloat16)
        return carry

    lax.fori_loop(0, width // D_HEAD, head_body, 0)


def attend(bias, q, k, v, do, shared, prev):
    rows, width = q.shape
    bf = jnp.bfloat16
    vmem = pl.BlockSpec(memory_space=pltpu.VMEM)
    both = jax.ShapeDtypeStruct((2 * rows, width), bf)
    return pl.pallas_call(
        attend_kernel,
        out_shape=[jax.ShapeDtypeStruct((rows, width), bf), both, both, both],
        in_specs=[pl.BlockSpec(memory_space=pltpu.SMEM)] + [vmem] * 6,
        out_specs=[vmem] * 4,
        scratch_shapes=[
            pltpu.VMEM((3 * rows, D_HEAD), bf),
            pltpu.VMEM((3 * rows, D_HEAD), bf),
            pltpu.VMEM((3 * rows, rows), jnp.float32),
            pltpu.VMEM((3 * rows, rows), jnp.float32),
            pltpu.VMEM((3 * rows, rows), bf),
            pltpu.VMEM((3 * rows, rows), bf),
        ],
        compiler_params=pltpu.CompilerParams(vmem_limit_bytes=VMEM_LIMIT),
        name="attend",
    )(bias, q, k, v, do, shared, prev)


def sum_fill(chain, own, per_head, hops):
    last = chain.chunks - 1

    def mine(t):
        return chunk_of(own, jnp.clip(t, 0, last), per_head)[...]

    def fill(t, stage):
        @pl.when(t < LAG)
        def _():
            stage[...] = mine(t)

        @pl.when(t >= LAG)
        def _():
            added = chain.slots[t - LAG] + lax.select(hops == 2, mine(t - LAG), mine(t - 2 * LAG))
            stage[...] = lax.select(hops == 3, mine(t), added)

    return fill


def return_kernel(
    first_ref, own_ref, share_ref, back_hbm,
    dk_ref, dv_ref,
    returned, part,
    slots_z, slots_x, stage_z, stage_x,
    back_send, back_recv, z_send, z_recv, x_send, x_recv,
):
    at = Place()
    rows, width = dk_ref.shape
    per_head = 2 * rows // CHUNK
    chunks = per_head * (width // D_HEAD)
    meet([at.after, at.before, at.zup, at.zdown, at.xup, at.xdown])
    back = remote(back_hbm, returned, back_send, back_recv, at.before)
    back.start()
    first = first_ref[0]
    hops_x = (first // SIDE - at.x) & (SIDE - 1)
    hops_z = (first % SIDE - at.z) & (SIDE - 1)
    mine = lax.select(first == at.tm, jnp.float32(1), jnp.float32(0))
    chain_z = Chain(slots_z, stage_z, z_send, z_recv, at.zup, chunks)
    chain_x = Chain(slots_x, stage_x, x_send, x_recv, at.xup, chunks)
    fill_z = sum_fill(chain_z, share_ref, per_head, hops_z)
    fill_x = sum_fill(chain_x, part, per_head, hops_x)

    def chain_step(t, carry):
        chain_z.step(t, fill_z)
        u = t - 3 * LAG

        @pl.when((u >= 0) & (u < chunks))
        def _():
            here = chunk_of(share_ref, u, per_head)[...]
            chunk_of(part, u, per_head)[...] = here + slots_z[u + 2 * LAG]

        chain_x.step(u, fill_x)
        w = u - 3 * LAG

        @pl.when(w >= 0)
        def _():
            here = chunk_of(part, w, per_head)
            here[...] = here[...] + slots_x[w + 2 * LAG]

        return carry

    lax.fori_loop(0, chunks + 6 * LAG, chain_step, 0)
    back.wait_recv()
    back.wait_send()
    chain_z.drain()
    chain_x.drain()
    f32 = jnp.float32
    for out, start in ((dk_ref, 0), (dv_ref, rows)):
        for r in range(0, rows, 112):
            span = pl.ds(start + r, 112)
            full = own_ref[span, :].astype(f32) + returned[span, :].astype(f32)
            full = full + lax.select(
                mine > 0.5, part[span, :].astype(f32), jnp.zeros((112, width), f32)
            )
            out[pl.ds(r, 112), :] = full.astype(out.dtype)


def give_back(first_group, own, share, back):
    rows2, width = own.shape
    rows = rows2 // 2
    chunks = (rows2 // CHUNK) * (width // D_HEAD)
    steps = chunks + 2 * LAG
    bf = jnp.bfloat16
    dma = pltpu.SemaphoreType.DMA
    vmem = pl.BlockSpec(memory_space=pltpu.VMEM)
    out = jax.ShapeDtypeStruct((rows, width), bf)
    return pl.pallas_call(
        return_kernel,
        out_shape=[out, out],
        in_specs=[pl.BlockSpec(memory_space=pltpu.SMEM), vmem, vmem, pl.BlockSpec(memory_space=pl.ANY)],
        out_specs=[vmem, vmem],
        scratch_shapes=[
            pltpu.VMEM((rows2, width), bf),
            pltpu.VMEM((rows2, width), bf),
            pltpu.VMEM((steps, CHUNK, D_HEAD), bf),
            pltpu.VMEM((steps, CHUNK, D_HEAD), bf),
            pltpu.VMEM((SLOTS, CHUNK, D_HEAD), bf),
            pltpu.VMEM((SLOTS, CHUNK, D_HEAD), bf),
            dma, dma,
            dma((SLOTS,)), dma((steps,)), dma((SLOTS,)), dma((steps,)),
        ],
        compiler_params=pltpu.CompilerParams(
            collective_id=1, has_side_effects=True, vmem_limit_bytes=VMEM_LIMIT
        ),
        name="give_back",
    )(first_group, own, share, back)


def local(query_in, key_in, value_in, layer_grad, out_weight, group_mask, first_group):
    me = lax.axis_index("tm")
    first = first_group[0]
    before = jnp.maximum(me - 1, 0)
    prev_used = (me > 0) & (group_mask[me, before] == 1) & (first != me - 1)
    used = jnp.stack([jnp.bool_(True), first != me, prev_used])
    bias = jnp.where(used, 0.0, LOWEST).astype(jnp.float32)
    do, shared, prev = gather(first_group, layer_grad, out_weight, key_in, value_in)
    dq, own, share, back = attend(bias, query_in, key_in, value_in, do, shared, prev)
    dk, dv = give_back(first_group, own, share, back)
    return dq, dk, dv


def solution(mesh):
    tiles = P("tm", "head")
    return jax.shard_map(
        local,
        mesh=mesh,
        in_specs=(tiles, tiles, tiles, tiles, P("head", None), P(), P()),
        out_specs=(tiles, tiles, tiles),
        check_vma=False,
    )
```

time: 419 us -> 274 us (0.65); the launches traced: 412 us -> 271 us
  Pallas kernels: 0 us -> 264 us
  waiting for transfers between devices: 210 us -> 0 us
  matrix products: 90.6 us -> 0 us
  local copies, waits for them, and re-layouts: 41.6 us -> 4.56 us
  other arithmetic: 34.2 us -> 0.59 us
  between operations: 17.3 us -> 1.98 us
  loops' own time: 11.2 us -> 0 us
  starting transfers between devices: 6.6 us -> 0 us
    pallas_call x0 -> x3, Pallas kernels: none -> 264 us  [the longest x1 91.8 us: gather(): pl.pallas_call(gather_kernel, out_shape=[jax.ShapeDtypeStruct((rows, widt...]
    psum x2 -> x0, waiting for transfers between devices: 210 us -> none  [the longest x1 105 us: local(): lax.psum(first_key.astype(jnp.bfloat16), 'tm').astype(jnp.float32)]
    dot_general x13 -> x0, matrix products: 90.6 us -> none  [the longest x2 20.6 us: pair_grads(): jnp.einsum('qhd,khd->hqk', grad_blk, value_blk, preferred_element_type=jn...]
    convert_element_type x4 -> x0, other arithmetic: 19.2 us -> none  [the longest x1 10.2 us: pair_grads(): dscores = (probs * (dprobs - deltas[:, :, None])).astype(jnp.bfloat16)]
    another operation x4 -> x0, loops' own time: 11.2 us -> none  [the longest x1 10.4 us: local(): lax.cond(prev_used, lambda: pair_grads(query_three, grad_three, log_sums,...]
    slice x6 -> x0, local copies, waits for them, and re-layouts: 11.1 us -> none  [the longest x2 5.05 us: local(): prev_values = split_heads(prev_pair[1], head_dim)]
    unnamed x28 -> x4, local copies, waits for them, and re-layouts: 13.2 us -> 3.29 us
    reduce_sum x1 -> x0, other arithmetic: 7.36 us -> none  [pair_stats(): return (peak, jnp.sum(weights, axis=2), jnp.sum(weights * dprobs, axis=2))]
  transfers between devices with their start and end apart: 5 -> 0, of which waited for: 2 -> 0; matrix products, arithmetic and copies ran while one was open for 21% -> 0% of each run, Pallas kernels for 0% -> 0%
where the time goes in v1:
time: 274 us; the launch traced here: 271 us
  Pallas kernels  264 us (96%)
  local copies, waits for them, and re-layouts  4.56 us (2%)
    pallas_call x1, Pallas kernels, gather(): pl.pallas_call(gather_kernel, out_shape=[jax.ShapeDtypeStruct((rows, widt...  91.8 us
    pallas_call x1, Pallas kernels, give_back(): pl.pallas_call(return_kernel, out_shape=[out, out], in_specs=[pl.BlockSpe...  89.8 us
    pallas_call x1, Pallas kernels, attend(): pl.pallas_call(attend_kernel, out_shape=[jax.ShapeDtypeStruct((rows, widt...  82.8 us

profile of v1, /device:TPU:0, one launch (start us, length us, event | category | flops | bytes accessed | tf_op | source)
XLA Modules:
  0.0 271.5 jit_solution(4181546576785540964)
XLA Ops:
  1.3 1.3 dynamic_slice.3
  3.2 0.6 add_select_fusion.bias_ref
  3.8 91.8 %gather.1 = (bf16[784,640]{1,0:T(8,128)(2,1)}, bf16[1568,640]{1,0:T(8,128)(2,1)}, bf16[2,784,640]{2,1,0:T(8,128)(2,1)}) custom-call(s32[1]{0:T(128)} %copy.12.first_ref, bf16[784,640]{1,0:T(8,128)(2,1)} %g_hbm.1, bf16[640,5120]{1,0:T(8,128)(2,1)} %w_hbm.1, bf16[784,640]{1,0:T(8,128)(2,1)} %k_ref.1, bf16[784,640]{1,0:T(8,128)(2,1)} %v_ref.1), custom_call_target="tpu_custom_call" | custom-call | tf_op jit(solution)/shard_map/gather/pallas_call | solution.py:267
  95.6 82.8 %attend.1 = (bf16[784,640]{1,0:T(8,128)(2,1)}, bf16[1568,640]{1,0:T(8,128)(2,1)}, bf16[1568,640]{1,0:T(8,128)(2,1)}, bf16[1568,640]{1,0:T(8,128)(2,1)}) custom-call(f32[3]{0:T(128)} %add_select_fusion.bias_ref, bf16[784,640]{1,0:T(8,128)(2,1)} %q_ref.1, bf16[784,640]{1,0:T(8,128)(2,1)} %k_ref.1, bf16[784,640]{1,0:T(8,128)(2,1)} %v_ref.1, ...), custom_call_target="tpu_custom_call" | custom-call | tf_op jit(solution)/shard_map/attend/pallas_call | solution.py:370
  178.4 89.8 %give_back.1 = (bf16[784,640]{1,0:T(8,128)(2,1)}, bf16[784,640]{1,0:T(8,128)(2,1)}) custom-call(s32[1]{0:T(128)} %copy.12.first_ref, bf16[1568,640]{1,0:T(8,128)(2,1)} %get-tuple-element.16.own_ref, bf16[1568,640]{1,0:T(8,128)(2,1)} %get-tuple-element.17.share_ref, bf16[1568,640]{1,0:T(8,128)(2,1)} %get-tuple-element.18.back_hbm), custom_call_target="tpu_custom_call" | custom-call | tf_op jit(solution)/shard_map/give_back/pallas_call | solution.py:474
  268.2 0.0 copy-start
  268.2 2.3 copy.13
  270.5 0.0 copy-done
  270.5 1.0 copy.14
Async XLA Ops:
  268.2 2.3 copy-start

commit v2 on v0

v2 whole, which is shorter than its diff:
```python
import functools
import math

import jax
import jax.numpy as jnp
from jax import lax
from jax.experimental import pallas as pl
from jax.experimental.pallas import tpu as pltpu
from jax.sharding import PartitionSpec as P

MESH = pl.DeviceIdType.MESH
D_HEAD = 128
SIDE = 4
CHUNK = 224
LAG = 3
SLOTS = 6
ROW_CUT = 400
VMEM_LIMIT = 63 * 1024 * 1024
LOWEST = -1e30
NT = (((1,), (1,)), ((), ()))
NN = (((1,), (0,)), ((), ()))


class Place:
    def __init__(self):
        tm, head = lax.axis_index("tm"), lax.axis_index("head")
        self.tm, self.head = tm, head
        x, z = tm // SIDE, tm % SIDE
        self.x, self.z = x, z
        self.sib_head = head + 1 - 2 * (head % 2)
        self.up_head = (head + 2) % 8
        self.down_head = (head + 6) % 8
        self.far_head = (head + 4) % 8
        self.sib = (tm, self.sib_head)
        self.up = (tm, self.up_head)
        self.down = (tm, self.down_head)
        self.after = ((tm + 1) % 16, head)
        self.before = ((tm + 15) % 16, head)
        self.zup = (x * SIDE + (z + 1) % SIDE, head)
        self.zdown = (x * SIDE + (z + 3) % SIDE, head)
        self.xup = (((x + 1) % SIDE) * SIDE + z, head)
        self.xdown = (((x + 3) % SIDE) * SIDE + z, head)


def meet(peers):
    barrier = pltpu.get_barrier_semaphore()
    for peer in peers:
        pl.semaphore_signal(barrier, inc=1, device_id=peer, device_id_type=MESH)
    pl.semaphore_wait(barrier, len(peers))


def remote(src, dst, send, recv, peer):
    return pltpu.make_async_remote_copy(
        src_ref=src, dst_ref=dst, send_sem=send, recv_sem=recv, device_id=peer, device_id_type=MESH
    )


def chunk_of(ref, c, per_head):
    rows = pl.ds(pl.multiple_of((c % per_head) * CHUNK, CHUNK), CHUNK)
    cols = pl.ds(pl.multiple_of((c // per_head) * D_HEAD, D_HEAD), D_HEAD)
    return ref.at[rows, cols]


class Chain:
    def __init__(self, slots, stage, send, recv, peer, chunks):
        self.slots, self.stage, self.send, self.recv = slots, stage, send, recv
        self.peer, self.chunks = peer, chunks
        self.steps = chunks + 2 * LAG

    def copy(self, t):
        s = lax.rem(t, SLOTS)
        return remote(
            self.stage.at[s], self.slots.at[t], self.send.at[s], self.recv.at[t], self.peer
        )

    def step(self, t, fill):
        @pl.when((t >= LAG) & (t < self.steps + LAG))
        def _():
            self.copy(t - LAG).wait_recv()

        @pl.when((t >= 0) & (t < self.steps))
        def _():
            @pl.when(t >= SLOTS)
            def _():
                self.copy(t - SLOTS).wait_send()

            fill(t, self.stage.at[lax.rem(t, SLOTS)])
            self.copy(t).start()

    def drain(self):
        def one(t, carry):
            self.copy(t).wait_send()
            return carry

        lax.fori_loop(self.steps - SLOTS, self.steps, one, 0)


def spread_fill(chain, own, per_head, at_root):
    def fill(t, stage):
        mine = chunk_of(own, jnp.minimum(t, chain.chunks - 1), per_head)

        @pl.when(t < LAG)
        def _():
            stage[...] = mine[...]

        @pl.when(t >= LAG)
        def _():
            stage[...] = lax.select(at_root, mine[...], chain.slots[t - LAG])

    return fill


def spread_result(chain, u, own, hops):
    near = lax.select(hops == 0, own, chain.slots[u])
    far = lax.select(hops == 2, chain.slots[u + LAG], chain.slots[u + 2 * LAG])
    return lax.select(hops < 2, near, far)


def sum_fill(chain, own, per_head, hops):
    last = chain.chunks - 1

    def mine(t):
        return chunk_of(own, jnp.clip(t, 0, last), per_head)[...]

    def fill(t, stage):
        @pl.when(t < LAG)
        def _():
            stage[...] = mine(t)

        @pl.when(t >= LAG)
        def _():
            added = chain.slots[t - LAG] + lax.select(hops == 2, mine(t - LAG), mine(t - 2 * LAG))
            stage[...] = lax.select(hops == 3, mine(t), added)

    return fill


def fused_kernel(
    first_ref, bias_ref, q_hbm, k_hbm, v_hbm, g_hbm, w_hbm,
    dq_ref, dk_ref, dv_ref,
    gathered, weight, q_ref, kv, do_ref, shared, prev, share, back, returned,
    scores, dprobs, keys_t, dq_t,
    in_x, in_z, in_stage_x, in_stage_z, out_x, out_z, out_stage_x, out_stage_z,
    load_sem, side_send, side_recv, up_send, up_recv, down_send, down_recv,
    prev_send, prev_recv, back_send, back_recv,
    ix_send, ix_recv, iz_send, iz_recv, ox_send, ox_recv, oz_send, oz_recv,
):
    at = Place()
    f32, bf = jnp.float32, jnp.bfloat16
    rows, width = q_ref.shape
    heads = width // D_HEAD
    per_head = 2 * rows // CHUNK
    chunks = per_head * heads
    end = chunks + 6 * LAG
    loads = [
        pltpu.make_async_copy(g_hbm, gathered.at[at.head], load_sem.at[0]),
        pltpu.make_async_copy(k_hbm, kv.at[pl.ds(0, rows)], load_sem.at[1]),
        pltpu.make_async_copy(v_hbm, kv.at[pl.ds(rows, rows)], load_sem.at[2]),
        pltpu.make_async_copy(w_hbm, weight, load_sem.at[3]),
        pltpu.make_async_copy(q_hbm, q_ref, load_sem.at[4]),
    ]
    for load in loads:
        load.start()
    meet([at.sib, at.up, at.down, at.after, at.before, at.zup, at.zdown, at.xup, at.xdown])

    top, low = pl.ds(0, ROW_CUT), pl.ds(ROW_CUT, rows - ROW_CUT)
    every = pl.ds(0, rows)
    side, up, down = (side_send, side_recv), (up_send, up_recv), (down_send, down_recv)
    started = []

    def send(head, part, sems, n, peer):
        block = gathered.at[head, part]
        return remote(block, block, sems[0].at[n], sems[1].at[n], peer)

    def go(*args):
        copy = send(*args)
        copy.start()
        started.append(copy)

    def head_cols(h):
        return pl.ds(pl.multiple_of(h * D_HEAD, D_HEAD), D_HEAD)

    def prev_copy(h):
        span = (pl.ds(0, 2 * rows), head_cols(h))
        return remote(kv.at[span], prev.at[span], prev_send.at[h], prev_recv.at[h], at.after)

    def back_copy(h):
        span = (pl.ds(0, 2 * rows), head_cols(h))
        return remote(back.at[span], returned.at[span], back_send.at[h], back_recv.at[h], at.before)

    loads[0].wait()
    go(at.head, top, up, 0, at.up)
    go(at.head, low, down, 0, at.down)
    go(at.head, low, up, 1, at.up)
    go(at.head, top, down, 1, at.down)
    go(at.head, every, side, 0, at.sib)
    loads[1].wait()
    loads[2].wait()
    for h in range(heads):
        prev_copy(h).start()

    first = first_ref[0]
    hops_x = (first // SIDE - at.x) & (SIDE - 1)
    hops_z = (first % SIDE - at.z) & (SIDE - 1)
    spread_x = Chain(in_x, in_stage_x, ix_send, ix_recv, at.xdown, chunks)
    spread_z = Chain(in_z, in_stage_z, iz_send, iz_recv, at.zdown, chunks)
    sum_z = Chain(out_z, out_stage_z, oz_send, oz_recv, at.zup, chunks)
    sum_x = Chain(out_x, out_stage_x, ox_send, ox_recv, at.xup, chunks)
    spread_fill_x = spread_fill(spread_x, kv, per_head, hops_x == 0)
    spread_fill_z = spread_fill(spread_z, shared, per_head, hops_z == 0)
    sum_fill_z = sum_fill(sum_z, share, per_head, hops_z)
    sum_fill_x = sum_fill(sum_x, share, per_head, hops_x)

    def inside(u):
        return (u >= 0) & (u < chunks)

    def spread_step(t):
        spread_x.step(t, spread_fill_x)
        u = t - 3 * LAG
        w = u - 3 * LAG

        @pl.when(inside(u))
        def _():
            mine = chunk_of(kv, u, per_head)[...]
            chunk_of(shared, u, per_head)[...] = spread_result(spread_x, u, mine, hops_x)

        spread_z.step(u, spread_fill_z)

        @pl.when(inside(w))
        def _():
            mine = chunk_of(shared, w, per_head)
            mine[...] = spread_result(spread_z, w, mine[...], hops_z)

    def sum_step(t):
        sum_z.step(t, sum_fill_z)
        u = t - 3 * LAG
        w = u - 3 * LAG

        @pl.when(inside(u))
        def _():
            here = chunk_of(share, u, per_head)
            here[...] = here[...] + out_z[u + 2 * LAG]

        sum_x.step(u, sum_fill_x)

        @pl.when(inside(w))
        def _():
            here = chunk_of(share, w, per_head)
            here[...] = here[...] + out_x[w + 2 * LAG]

    def run(step, start, count):
        def one(i, carry):
            step(start + i)
            return carry

        lax.fori_loop(0, count, one, 0)

    total = scores.at[0, :, pl.ds(0, width)]

    def project(head, fresh=False):
        cols = pl.ds(pl.multiple_of(head * width, width), width)
        part = lax.dot_general(gathered[head], weight[:, cols], NT, preferred_element_type=f32)
        total[...] = part if fresh else total[...] + part

    run(spread_step, 0, 3)
    loads[3].wait()
    loads[4].wait()
    project(at.head, fresh=True)
    run(spread_step, 3, 2)
    send(at.sib_head, every, side, 0, at.sib).wait_recv()
    project(at.sib_head)
    run(spread_step, 5, 4)
    send(at.down_head, top, up, 0, at.up).wait_recv()
    go(at.down_head, top, up, 2, at.up)
    go(at.down_head, top, side, 1, at.sib)
    send(at.up_head, low, down, 0, at.down).wait_recv()
    go(at.up_head, low, down, 2, at.down)
    go(at.up_head, low, side, 2, at.sib)
    run(spread_step, 9, 9)
    send(at.down_head, low, up, 1, at.up).wait_recv()
    go(at.down_head, low, side, 3, at.sib)
    send(at.up_head, top, down, 1, at.down).wait_recv()
    go(at.up_head, top, side, 4, at.sib)
    project(at.down_head)
    run(spread_step, 18, 1)
    project(at.up_head)
    run(spread_step, 19, 2)
    down_sib, up_sib, far_sib = [
        h + 1 - 2 * (h % 2) for h in (at.down_head, at.up_head, at.far_head)
    ]
    send(down_sib, top, side, 1, at.sib).wait_recv()
    send(down_sib, low, side, 3, at.sib).wait_recv()
    project(down_sib)
    run(spread_step, 21, 1)
    send(up_sib, low, side, 2, at.sib).wait_recv()
    send(up_sib, top, side, 4, at.sib).wait_recv()
    project(up_sib)
    run(spread_step, 22, 5)
    send(at.far_head, top, up, 2, at.up).wait_recv()
    go(at.far_head, top, side, 5, at.sib)
    send(at.far_head, low, down, 2, at.down).wait_recv()
    go(at.far_head, low, side, 6, at.sib)
    project(at.far_head)
    run(spread_step, 27, 2)
    send(far_sib, top, side, 5, at.sib).wait_recv()
    send(far_sib, low, side, 6, at.sib).wait_recv()
    project(far_sib)
    do_ref[...] = total[...].astype(bf)
    for copy in started:
        copy.wait_send()
    run(spread_step, 29, 3)

    scale = D_HEAD ** (-0.5)
    unit = scale * math.log2(math.e)
    keys = (kv.at[pl.ds(0, rows)], shared.at[pl.ds(0, rows)], prev.at[pl.ds(0, rows)])
    values = (kv.at[pl.ds(rows, rows)], shared.at[pl.ds(rows, rows)], prev.at[pl.ds(rows, rows)])

    def head_body(h, carry):
        cols = head_cols(h)
        q, do = q_ref[:, cols], do_ref[:, cols]
        prev_copy(h).wait_recv()
        peak = jnp.full((1, rows), LOWEST, f32)
        for i in range(3):
            block = keys[i][:, cols]
            s = lax.dot_general(block, q, NT, preferred_element_type=f32)
            scores[i] = s
            peak = jnp.maximum(peak, jnp.max(s, axis=0, keepdims=True) + bias_ref[i])
            keys_t[:, i * rows : (i + 1) * rows] = jnp.transpose(block)
        run(spread_step, 32 + 7 * h, 2)
        run(sum_step, 7 * h - 5, 2)
        mass = jnp.zeros((1, rows), f32)
        dot = mass
        for i in range(3):
            dp = lax.dot_general(values[i][:, cols], do, NT, preferred_element_type=f32)
            e = jnp.exp2(scores[i] * unit - (peak * unit - bias_ref[i]))
            scores[i] = e
            dprobs[i] = dp
            mass += jnp.sum(e, axis=0, keepdims=True)
            dot += jnp.sum(e * dp, axis=0, keepdims=True)
        inverse = 1.0 / mass
        delta = dot * inverse
        run(spread_step, 34 + 7 * h, 2)
        run(sum_step, 7 * h - 3, 2)

        def grads(i):
            p = scores[i] * inverse
            ds = (p * (dprobs[i] - delta)).astype(bf)
            dv = lax.dot_general(p.astype(bf), do, NN, preferred_element_type=f32)
            dk = lax.dot_general(ds, q, NN, preferred_element_type=f32)
            dq = lax.dot_general(
                keys_t[:, i * rows : (i + 1) * rows], ds, NN, preferred_element_type=f32
            )
            return (dk * scale).astype(bf), dv.astype(bf), dq

        share[0:rows, cols], share[rows : 2 * rows, cols], dq_t[...] = grads(1)
        run(spread_step, 36 + 7 * h, 1)
        run(sum_step, 7 * h - 1, 2)
        back[0:rows, cols], back[rows : 2 * rows, cols], dq = grads(2)
        back_copy(h).start()
        dq_t[...] += dq
        run(spread_step, 37 + 7 * h, 1)
        run(sum_step, 7 * h + 1, 1)
        dk_ref[:, cols], dv_ref[:, cols], dq = grads(0)
        dq_ref[:, cols] = (jnp.transpose(dq_t[...] + dq) * scale).astype(bf)
        run(spread_step, 38 + 7 * h, 1)
        return carry

    lax.fori_loop(0, heads, head_body, 0)
    done = 7 * heads - 5
    run(sum_step, done, end - done)
    for h in range(heads):
        back_copy(h).wait_recv()
    mine = first == at.tm
    for out, start in ((dk_ref, 0), (dv_ref, rows)):
        for r in range(0, rows, 112):
            span, here = pl.ds(start + r, 112), pl.ds(r, 112)
            full = out[here, :].astype(f32) + returned[span, :].astype(f32)
            full = full + lax.select(mine, share[span, :].astype(f32), jnp.zeros((112, width), f32))
            out[here, :] = full.astype(bf)
    for h in range(heads):
        prev_copy(h).wait_send()
        back_copy(h).wait_send()
    for chain in (spread_x, spread_z, sum_z, sum_x):
        chain.drain()


def fused(first_group, bias, q, k, v, g, w):
    rows, width = q.shape
    heads = width // D_HEAD
    chunks = (2 * rows // CHUNK) * heads
    steps = chunks + 2 * LAG
    bf = jnp.bfloat16
    dma = pltpu.SemaphoreType.DMA
    smem = pl.BlockSpec(memory_space=pltpu.SMEM)
    anywhere = pl.BlockSpec(memory_space=pl.ANY)
    vmem = pl.BlockSpec(memory_space=pltpu.VMEM)
    out = jax.ShapeDtypeStruct((rows, width), bf)
    both = pltpu.VMEM((2 * rows, width), bf)
    slots = pltpu.VMEM((steps, CHUNK, D_HEAD), bf)
    stage = pltpu.VMEM((SLOTS, CHUNK, D_HEAD), bf)
    return pl.pallas_call(
        fused_kernel,
        out_shape=[out] * 3,
        in_specs=[smem] * 2 + [anywhere] * 5,
        out_specs=[vmem] * 3,
        scratch_shapes=[
            pltpu.VMEM((8, rows, width), bf),
            pltpu.VMEM(w.shape, bf),
            pltpu.VMEM((rows, width), bf),
            both,
            pltpu.VMEM((rows, width), bf),
            both, both, both, both, both,
            pltpu.VMEM((3, rows, rows), jnp.float32),
            pltpu.VMEM((3, rows, rows), jnp.float32),
            pltpu.VMEM((D_HEAD, 3 * rows), bf),
            pltpu.VMEM((D_HEAD, rows), jnp.float32),
            slots, slots, stage, stage, slots, slots, stage, stage,
            dma((5,)),
            dma((7,)), dma((7,)), dma((3,)), dma((3,)), dma((3,)), dma((3,)),
            dma((heads,)), dma((heads,)), dma((heads,)), dma((heads,)),
        ]
        + [dma((SLOTS,)), dma((steps,))] * 4,
        compiler_params=pltpu.CompilerParams(
            collective_id=0, has_side_effects=True, vmem_limit_bytes=VMEM_LIMIT
        ),
        name="fused",
    )(first_group, bias, q, k, v, g, w)


def local(query_in, key_in, value_in, layer_grad, out_weight, group_mask, first_group):
    me = lax.axis_index("tm")
    first = first_group[0]
    before = jnp.maximum(me - 1, 0)
    prev_used = (me > 0) & (group_mask[me, before] == 1) & (first != me - 1)
    used = jnp.stack([jnp.bool_(True), first != me, prev_used])
    bias = jnp.where(used, 0.0, LOWEST).astype(jnp.float32)
    dq, dk, dv = fused(first_group, bias, query_in, key_in, value_in, layer_grad, out_weight)
    return dq, dk, dv


def solution(mesh):
    tiles = P("tm", "head")
    return jax.shard_map(
        local,
        mesh=mesh,
        in_specs=(tiles, tiles, tiles, tiles, P("head", None), P(), P()),
        out_specs=(tiles, tiles, tiles),
        check_vma=False,
    )
```

time: 419 us -> 168 us (0.40); the launches traced: 412 us -> 168 us
  waiting for transfers between devices: 210 us -> 0 us
  Pallas kernels: 0 us -> 157 us
  matrix products: 90.6 us -> 0 us
  other arithmetic: 34.2 us -> 0.59 us
  local copies, waits for them, and re-layouts: 41.6 us -> 8.01 us
  between operations: 17.3 us -> 1.96 us
  loops' own time: 11.2 us -> 0 us
  starting transfers between devices: 6.6 us -> 0 us
    psum x2 -> x0, waiting for transfers between devices: 210 us -> none  [the longest x1 105 us: local(): lax.psum(first_key.astype(jnp.bfloat16), 'tm').astype(jnp.float32)]
    pallas_call x0 -> x1, Pallas kernels: none -> 157 us  [fused(): pl.pallas_call(fused_kernel, out_shape=[out] * 3, in_specs=[smem] * 2 + [...]
    dot_general x13 -> x0, matrix products: 90.6 us -> none  [the longest x2 20.6 us: pair_grads(): jnp.einsum('qhd,khd->hqk', grad_blk, value_blk, preferred_element_type=jn...]
    convert_element_type x4 -> x0, other arithmetic: 19.2 us -> none  [the longest x1 10.2 us: pair_grads(): dscores = (probs * (dprobs - deltas[:, :, None])).astype(jnp.bfloat16)]
    another operation x4 -> x0, loops' own time: 11.2 us -> none  [the longest x1 10.4 us: local(): lax.cond(prev_used, lambda: pair_grads(query_three, grad_three, log_sums,...]
    slice x6 -> x0, local copies, waits for them, and re-layouts: 11.1 us -> none  [the longest x2 5.05 us: local(): prev_values = split_heads(prev_pair[1], head_dim)]
    reduce_sum x1 -> x0, other arithmetic: 7.36 us -> none  [pair_stats(): return (peak, jnp.sum(weights, axis=2), jnp.sum(weights * dprobs, axis=2))]
    convert_element_type x4 -> x0, local copies, waits for them, and re-layouts: 6.78 us -> none  [the longest x1 2.01 us: local(): query_out = query_acc.reshape(rows_loc, width_loc).astype(jnp.bfloat16)]
  transfers between devices with their start and end apart: 5 -> 0, of which waited for: 2 -> 0; matrix products, arithmetic and copies ran while one was open for 21% -> 0% of each run, Pallas kernels for 0% -> 0%
where the time goes in v2:
time: 168 us
  Pallas kernels  157 us (93%)
  local copies, waits for them, and re-layouts  8.01 us (5%)
  between operations  1.96 us (1%)
    pallas_call x1, Pallas kernels, fused(): pl.pallas_call(fused_kernel, out_shape=[out] * 3, in_specs=[smem] * 2 + [...  157 us
    unnamed x3, local copies, waits for them, and re-layouts  6.74 us

profile of v2, /device:TPU:0, one launch (start us, length us, event | category | flops | bytes accessed | tf_op | source)
XLA Modules:
  0.0 167.9 jit_solution(11484172403675651511)
XLA Ops:
  1.3 1.3 dynamic_slice.3
  3.2 0.6 add_select_fusion.bias_ref
  3.8 157.3 %fused.1 = (bf16[784,640]{1,0:T(8,128)(2,1)}, bf16[784,640]{1,0:T(8,128)(2,1)}, bf16[784,640]{1,0:T(8,128)(2,1)}) custom-call(s32[1]{0:T(128)} %copy.13.first_ref, f32[3]{0:T(128)} %add_select_fusion.bias_ref, bf16[784,640]{1,0:T(8,128)(2,1)} %q_hbm.1, bf16[784,640]{1,0:T(8,128)(2,1)} %k_hbm.1, bf16[784,640]{1,0:T(8,128)(2,1)} %v_hbm.1, ...), custom_call_target="tpu_custom_call" | custom-call | tf_op jit(solution)/shard_map/fused/pallas_call | solution.py:401
  161.1 2.2 %copy.14 = bf16[784,640]{1,0:T(8,128)(2,1)} copy(bf16[784,640]{1,0:T(8,128)(2,1)} %get-tuple-element.6) | data formatting | bytes 2007040
  163.4 2.2 %copy.15 = bf16[784,640]{1,0:T(8,128)(2,1)} copy(bf16[784,640]{1,0:T(8,128)(2,1)} %get-tuple-element.7) | data formatting | bytes 2007040
  165.6 2.2 %copy.16 = bf16[784,640]{1,0:T(8,128)(2,1)} copy(bf16[784,640]{1,0:T(8,128)(2,1)} %get-tuple-element.8) | data formatting | bytes 2007040

commit v3 on v2

--- a/solution.py
+++ b/solution.py
@@ -17,6 +17,8 @@
 ROW_CUT = 400
 VMEM_LIMIT = 63 * 1024 * 1024
 LOWEST = -1e30
+BACK_LAG = 12
+FINISH_ROWS = 784
 NT = (((1,), (1,)), ((), ()))
 NN = (((1,), (0,)), ((), ()))
 
@@ -136,9 +138,9 @@
 
 
 def fused_kernel(
-    first_ref, bias_ref, q_hbm, k_hbm, v_hbm, g_hbm, w_hbm,
-    dq_ref, dk_ref, dv_ref,
-    gathered, weight, q_ref, kv, do_ref, shared, prev, share, back, returned,
+    first_ref, mask_ref, q_hbm, k_hbm, v_hbm, g_hbm, w_hbm,
+    dq_ref, own_ref, share, returned,
+    gathered, weight, q_ref, kv, do_ref, shared, prev, back,
     scores, dprobs, keys_t, dq_t,
     in_x, in_z, in_stage_x, in_stage_z, out_x, out_z, out_stage_x, out_stage_z,
     load_sem, side_send, side_recv, up_send, up_recv, down_send, down_recv,
@@ -184,9 +186,11 @@
         span = (pl.ds(0, 2 * rows), head_cols(h))
         return remote(kv.at[span], prev.at[span], prev_send.at[h], prev_recv.at[h], at.after)
 
-    def back_copy(h):
-        span = (pl.ds(0, 2 * rows), head_cols(h))
-        return remote(back.at[span], returned.at[span], back_send.at[h], back_recv.at[h], at.before)
+    def back_copy(c):
+        src, dst = chunk_of(back, c, per_head), chunk_of(returned, c, per_head)
+        return remote(src, dst, back_send, back_recv, at.before)
+
+    back_all = remote(back, returned, back_send, back_recv, at.before)
 
     loads[0].wait()
     go(at.head, top, up, 0, at.up)
@@ -200,6 +204,12 @@
         prev_copy(h).start()
 
     first = first_ref[0]
+    used = (mask_ref[at.tm, jnp.maximum(at.tm - 1, 0)] == 1) & (at.tm > 0) & (first != at.tm - 1)
+    bias = (
+        jnp.float32(0),
+        lax.select(first != at.tm, jnp.float32(0), jnp.float32(LOWEST)),
+        lax.select(used, jnp.float32(0), jnp.float32(LOWEST)),
+    )
     hops_x = (first // SIDE - at.x) & (SIDE - 1)
     hops_z = (first % SIDE - at.z) & (SIDE - 1)
     spread_x = Chain(in_x, in_stage_x, ix_send, ix_recv, at.xdown, chunks)
@@ -233,6 +243,7 @@
 
     def sum_step(t):
         sum_z.step(t, sum_fill_z)
+        pl.when(inside(t - BACK_LAG))(lambda: back_copy(t - BACK_LAG).start())
         u = t - 3 * LAG
         w = u - 3 * LAG
 
@@ -324,7 +335,7 @@
             block = keys[i][:, cols]
             s = lax.dot_general(block, q, NT, preferred_element_type=f32)
             scores[i] = s
-            peak = jnp.maximum(peak, jnp.max(s, axis=0, keepdims=True) + bias_ref[i])
+            peak = jnp.maximum(peak, jnp.max(s, axis=0, keepdims=True) + bias[i])
             keys_t[:, i * rows : (i + 1) * rows] = jnp.transpose(block)
         run(spread_step, 32 + 7 * h, 2)
         run(sum_step, 7 * h - 5, 2)
@@ -332,7 +343,7 @@
         dot = mass
         for i in range(3):
             dp = lax.dot_general(values[i][:, cols], do, NT, preferred_element_type=f32)
-            e = jnp.exp2(scores[i] * unit - (peak * unit - bias_ref[i]))
+            e = jnp.exp2(scores[i] * unit - (peak * unit - bias[i]))
             scores[i] = e
             dprobs[i] = dp
             mass += jnp.sum(e, axis=0, keepdims=True)
@@ -356,11 +367,10 @@
         run(spread_step, 36 + 7 * h, 1)
         run(sum_step, 7 * h - 1, 2)
         back[0:rows, cols], back[rows : 2 * rows, cols], dq = grads(2)
-        back_copy(h).start()
         dq_t[...] += dq
         run(spread_step, 37 + 7 * h, 1)
         run(sum_step, 7 * h + 1, 1)
-        dk_ref[:, cols], dv_ref[:, cols], dq = grads(0)
+        own_ref[0:rows, cols], own_ref[rows : 2 * rows, cols], dq = grads(0)
         dq_ref[:, cols] = (jnp.transpose(dq_t[...] + dq) * scale).astype(bf)
         run(spread_step, 38 + 7 * h, 1)
         return carry
@@ -368,23 +378,15 @@
     lax.fori_loop(0, heads, head_body, 0)
     done = 7 * heads - 5
     run(sum_step, done, end - done)
-    for h in range(heads):
-        back_copy(h).wait_recv()
-    mine = first == at.tm
-    for out, start in ((dk_ref, 0), (dv_ref, rows)):
-        for r in range(0, rows, 112):
-            span, here = pl.ds(start + r, 112), pl.ds(r, 112)
-            full = out[here, :].astype(f32) + returned[span, :].astype(f32)
-            full = full + lax.select(mine, share[span, :].astype(f32), jnp.zeros((112, width), f32))
-            out[here, :] = full.astype(bf)
+    back_all.wait_recv()
     for h in range(heads):
         prev_copy(h).wait_send()
-        back_copy(h).wait_send()
+    back_all.wait_send()
     for chain in (spread_x, spread_z, sum_z, sum_x):
         chain.drain()
 
 
-def fused(first_group, bias, q, k, v, g, w):
+def fused(first_group, group_mask, q, k, v, g, w):
     rows, width = q.shape
     heads = width // D_HEAD
     chunks = (2 * rows // CHUNK) * heads
@@ -395,21 +397,22 @@
     anywhere = pl.BlockSpec(memory_space=pl.ANY)
     vmem = pl.BlockSpec(memory_space=pltpu.VMEM)
     out = jax.ShapeDtypeStruct((rows, width), bf)
+    out2 = jax.ShapeDtypeStruct((2 * rows, width), bf)
     both = pltpu.VMEM((2 * rows, width), bf)
     slots = pltpu.VMEM((steps, CHUNK, D_HEAD), bf)
     stage = pltpu.VMEM((SLOTS, CHUNK, D_HEAD), bf)
     return pl.pallas_call(
         fused_kernel,
-        out_shape=[out] * 3,
+        out_shape=[out, out2, out2, out2],
         in_specs=[smem] * 2 + [anywhere] * 5,
-        out_specs=[vmem] * 3,
+        out_specs=[vmem] * 3 + [anywhere],
         scratch_shapes=[
             pltpu.VMEM((8, rows, width), bf),
             pltpu.VMEM(w.shape, bf),
             pltpu.VMEM((rows, width), bf),
             both,
             pltpu.VMEM((rows, width), bf),
-            both, both, both, both, both,
+            both, both, both,
             pltpu.VMEM((3, rows, rows), jnp.float32),
             pltpu.VMEM((3, rows, rows), jnp.float32),
             pltpu.VMEM((D_HEAD, 3 * rows), bf),
@@ -417,25 +420,51 @@
             slots, slots, stage, stage, slots, slots, stage, stage,
             dma((5,)),
             dma((7,)), dma((7,)), dma((3,)), dma((3,)), dma((3,)), dma((3,)),
-            dma((heads,)), dma((heads,)), dma((heads,)), dma((heads,)),
+            dma((heads,)), dma((heads,)), dma, dma,
         ]
         + [dma((SLOTS,)), dma((steps,))] * 4,
         compiler_params=pltpu.CompilerParams(
             collective_id=0, has_side_effects=True, vmem_limit_bytes=VMEM_LIMIT
         ),
         name="fused",
-    )(first_group, bias, q, k, v, g, w)
+    )(first_group, group_mask, q, k, v, g, w)
+
+
+def finish_kernel(
+    first_ref, dq_in, own_k, own_v, back_k, back_v, sum_k, sum_v, dq_ref, dk_ref, dv_ref
+):
+    f32 = jnp.float32
+    mine = first_ref[0] == lax.axis_index("tm")
+    dq_ref[...] = dq_in[...]
+    for out, own, back, total in ((dk_ref, own_k, back_k, sum_k), (dv_ref, own_v, back_v, sum_v)):
+        full = own[...].astype(f32) + back[...].astype(f32)
+        full = full + lax.select(mine, total[...].astype(f32), jnp.zeros(out.shape, f32))
+        out[...] = full.astype(out.dtype)
+
+
+def finish(first_group, dq, own, share, returned):
+    rows, width = dq.shape
+    step = FINISH_ROWS
+    blocks = rows // step
+    upper = pl.BlockSpec((step, width), lambda i: (i, 0))
+    lower = pl.BlockSpec((step, width), lambda i: (i + blocks, 0))
+    out = jax.ShapeDtypeStruct((rows, width), dq.dtype)
+    return pl.pallas_call(
+        finish_kernel,
+        grid=(blocks,),
+        out_shape=[out] * 3,
+        in_specs=[pl.BlockSpec(memory_space=pltpu.SMEM), upper] + [upper, lower] * 3,
+        out_specs=[upper] * 3,
+        compiler_params=pltpu.CompilerParams(vmem_limit_bytes=VMEM_LIMIT),
+        name="finish",
+    )(first_group, dq, own, own, returned, returned, share, share)
 
 
 def local(query_in, key_in, value_in, layer_grad, out_weight, group_mask, first_group):
-    me = lax.axis_index("tm")
-    first = first_group[0]
-    before = jnp.maximum(me - 1, 0)
-    prev_used = (me > 0) & (group_mask[me, before] == 1) & (first != me - 1)
-    used = jnp.stack([jnp.bool_(True), first != me, prev_used])
-    bias = jnp.where(used, 0.0, LOWEST).astype(jnp.float32)
-    dq, dk, dv = fused(first_group, bias, query_in, key_in, value_in, layer_grad, out_weight)
-    return dq, dk, dv
+    dq, own, share, returned = fused(
+        first_group, group_mask, query_in, key_in, value_in, layer_grad, out_weight
+    )
+    return tuple(finish(first_group, dq, own, share, returned))
 
 
 def solution(mesh):

time: 168 us -> 149 us (0.89)
  Pallas kernels: 157 us -> 147 us
  local copies, waits for them, and re-layouts: 8.01 us -> 0 us
    pallas_call x1 -> x2, Pallas kernels: 157 us -> 147 us  [the longest x1 142 us: fused(): pl.pallas_call(fused_kernel, out_shape=[out, out2, out2, out2], in_specs=...]
    unnamed x3 -> x0, local copies, waits for them, and re-layouts: 6.74 us -> none
where the time goes in v3:
time: 149 us
  Pallas kernels  147 us (99%)
    pallas_call x1, Pallas kernels, fused(): pl.pallas_call(fused_kernel, out_shape=[out, out2, out2, out2], in_specs=...  142 us
    pallas_call x1, Pallas kernels, finish(): pl.pallas_call(finish_kernel, grid=(blocks,), out_shape=[out] * 3, in_spe...  5.08 us

profile of v3, /device:TPU:0, one launch (start us, length us, event | category | flops | bytes accessed | tf_op | source)
XLA Modules:
  0.0 148.6 jit_solution(1952469493211665072)
XLA Ops:
  1.3 142.2 %fused.1 = (bf16[784,640]{1,0:T(8,128)(2,1)}, bf16[1568,640]{1,0:T(8,128)(2,1)}, bf16[1568,640]{1,0:T(8,128)(2,1)}, bf16[1568,640]{1,0:T(8,128)(2,1)}) custom-call(s32[1]{0:T(128)S(6)} %copy.10.first_ref, s32[16,16]{1,0:T(8,128)} %mask_ref.1, bf16[784,640]{1,0:T(8,128)(2,1)} %q_hbm.1, bf16[784,640]{1,0:T(8,128)(2,1)} %k_hbm.1, bf16[784,640]{1,0:T(8,128)(2,1)} %v_hbm.1, ...), custom_call_target="tpu_custom_call" | custom-call | tf_op jit(solution)/shard_map/fused/pallas_call | solution.py:404
  143.5 5.1 %finish.1 = (bf16[784,640]{1,0:T(8,128)(2,1)}, bf16[784,640]{1,0:T(8,128)(2,1)}, bf16[784,640]{1,0:T(8,128)(2,1)}) custom-call(s32[1]{0:T(128)S(6)} %copy.10.first_ref, bf16[784,640]{1,0:T(8,128)(2,1)} %get-tuple-element.7.dq_in, bf16[1568,640]{1,0:T(8,128)(2,1)} %get-tuple-element.8.own_k.own_v, bf16[1568,640]{1,0:T(8,128)(2,1)} %get-tuple-element.8.own_k.own_v, ...), custom_call_target="tpu_custom_call" | custom-call | tf_op jit(solution)/shard_map/finish/pallas_call | solution.py:452
